TPU v7x, 32 devices: a whole 2x2x4 slice. The times are simulated.
32 devices in a mesh: groups: 2 (over y), frame: 4 (over z), map: 2 (over x), psf: 2 (over core).
Axes of the slice: x: 2, y: 2, z: 4, core: 2. Of those that a mesh axis runs over, the one named last changes fastest.
Arguments:
- observed: float32 [8, 128, 512], P(('groups', 'frame'), ('map', 'psf')), parts along dimension 0, may hold values from -6 to 6
- pixel_mask: int32 [8, 128, 512], P(('groups', 'frame'), ('map', 'psf')), parts along dimension 0, may hold values 0 or 1
- ramp_counts: int32 [8, 128, 512], P(('groups', 'frame'), ('map', 'psf')), parts along dimension 0, may hold values from 1 to 16
- flat_map: float32 [8, 32, 512], P(('groups', 'map', 'psf'), 'frame'), parts along dimension 0, may hold values from 0.5 to 1.5
- bfe_map: float32 [8, 32, 512], P(('groups', 'map', 'psf'), 'frame'), parts along dimension 0, may hold values from 0.005 to 0.05
- ipc_kernel: float32 [6, 3], P('groups'), parts along dimension 0, may hold values from 0 to 0.04
- zernike: float32 [42], P('groups'), parts along dimension 0, may hold values from -2.5 to 2.5
- jitter: float32 [8], P(('groups', 'frame')), parts along dimension 0, may hold values from 4 to 20
- sky_level: float32 [8], P(('groups', 'frame')), parts along dimension 0, may hold values from 0.5 to 2
- dither: int32 [8, 2], P(('groups', 'frame')), parts along dimension 0, may hold values from -56 to 55
Outputs:
- grad_flat: float32 [8, 32, 512], P(('groups', 'map', 'psf'), 'frame'), parts along dimension 0
- grad_bfe: float32 [8, 32, 512], P(('groups', 'map', 'psf'), 'frame'), parts along dimension 0
- grad_ipc: float32 [6, 3], P('groups'), parts along dimension 0
- grad_zernike: float32 [42], P('groups'), parts along dimension 0
- grad_jitter: float32 [8], P(('groups', 'frame')), parts along dimension 0
There are 2 independent parts, one for each index of `groups`. A program takes and returns all parts, laid end to end along the dimension named above; each array names one. Nothing has to cross between parts.
All inputs are finite; a program needn't handle non-finite values. No bound on the sum of `pixel_mask` on one device may be relied on, other than what follows from the above.
Results may differ from a plain program's by a relative error of at most 0.0003.
Values sent between devices are 32-bit elements; how exact they have to be, the bound alone decides.
A program may use at most 64 MiB of HBM per device.

v0:
```python
import functools
import math

import jax
import jax.numpy as jnp
import numpy as np
from jax import lax
from jax.experimental import pallas as pl
from jax.experimental.pallas import tpu as pltpu
from jax.sharding import PartitionSpec as P

NP = 256
NR = 16
HALO = 8
OVERSAMPLE = 32
AMPLITUDE = 2.0
IPC_CENTER = 0.8
DEGREE = 5
F32 = jnp.float32
BF16 = jnp.bfloat16
MESH = pl.DeviceIdType.MESH


def turn_polynomials():
    nodes = 0.125 * (1.0 + np.cos((np.arange(64) + 0.5) * np.pi / 64))
    root = np.sqrt(nodes)
    cos_fit = np.polynomial.Chebyshev.fit(nodes, np.cos(2 * np.pi * root), 7, domain=[0, 0.25])
    sin_fit = np.polynomial.Chebyshev.fit(nodes, np.sin(2 * np.pi * root) / root, 7, domain=[0, 0.25])
    as_power = np.polynomial.Polynomial
    return (
        [float(v) for v in cos_fit.convert(kind=as_power).coef],
        [float(v) for v in sin_fit.convert(kind=as_power).coef],
    )


COS_COEF, SIN_COEF = turn_polynomials()


def horner(coefs, x):
    acc = jnp.full_like(x, coefs[-1])
    for value in coefs[-2::-1]:
        acc = acc * x + value
    return acc


def cos_sin_turns(turns):
    rest = turns - jnp.floor(turns + 0.5)
    square = rest * rest
    return horner(COS_COEF, square), rest * horner(SIN_COEF, square)


def bfe_weights():
    table = np.zeros((3, 3))
    total = 0.0
    for i in range(-2, 3):
        for j in range(-2, 3):
            if i or j:
                table[abs(i), abs(j)] = 1.0 / (i * i + j * j)
                total += 1.0 / (i * i + j * j)
    table[0, 0] = -total
    return (table / total).tolist()


BFE = bfe_weights()


def split(x):
    high = x.astype(BF16)
    return high, (x - high.astype(F32)).astype(BF16)


def mm(a, b, dims=((1,), (0,))):
    return lax.dot_general(a, b, (dims, ((), ())), preferred_element_type=F32)


def dot3(a, b_high, b_low, dims=((1,), (0,))):
    high, low = split(a)
    n = a.shape[0]
    both = mm(jnp.concatenate([high, low], 0), b_high, dims)
    return both[:n] + both[n:] + mm(high, b_low, dims)


def iota(shape, axis):
    return lax.broadcasted_iota(jnp.int32, shape, axis).astype(F32)


def repeat(count, body):
    if count <= 16:
        for i in range(count):
            body(i)
    else:
        lax.fori_loop(0, count, lambda i, c: (body(i), c)[1], 0)


def kernel(
    nf, nmap, npsf, rd, k, width,
    zern, jit, sky, dith, ipc, flat_in, bfe_in, obs_in, mask_in, count_in,
    gflat, gbfe, small,
    maps, ow, obs_v, mask_v, count_v, pup, ph, plo, bh, bl, gh, gl, dh, dl, gout, gin, outbox, inbox,
    local_sem, map_send, map_recv, ow_send, ow_recv, rs_send, rs_recv, box_send, box_recv,
):
    nb = nmap * npsf
    group = nf * nb
    rows = rd + 2 * HALO
    h = HALO // k
    f = lax.axis_index("frame")
    m = lax.axis_index("map")
    p = lax.axis_index("psf")
    b = m * npsf + p
    me = f * nb + b

    def device(frame, block):
        return {"frame": frame, "map": block // npsf, "psf": block % npsf}

    def peer(offset):
        other = lax.rem(me + offset, group)
        return other, device(other // nb, other % nb)

    barrier = pltpu.get_barrier_semaphore()

    def greet(i):
        pl.semaphore_signal(barrier, inc=1, device_id=peer(i + 1)[1], device_id_type=MESH)

    repeat(group - 1, greet)

    loads = [
        pltpu.make_async_copy(flat_in.at[0], maps.at[h + f, 0], local_sem.at[0]),
        pltpu.make_async_copy(bfe_in.at[0], maps.at[h + f, 1], local_sem.at[1]),
        pltpu.make_async_copy(obs_in.at[0], obs_v, local_sem.at[2]),
        pltpu.make_async_copy(mask_in.at[0], mask_v, local_sem.at[3]),
        pltpu.make_async_copy(count_in.at[0], count_v, local_sem.at[4]),
    ]
    for load in loads:
        load.start()

    step = 64
    lane_u = (2.0 * iota((1, NP), 1) + 1.0) / NP - 1.0
    lane_pow = [jnp.ones((1, NP), F32)]
    for _ in range(DEGREE):
        lane_pow.append(lane_pow[-1] * lane_u)
    per_power = []
    for power in range(DEGREE + 1):
        acc = jnp.zeros((1, NP), F32)
        for q in range(DEGREE + 1 - power):
            d = power + q
            acc = acc + (zern[d * (d + 1) // 2 + power] * (0.5 / math.pi)) * lane_pow[q]
        per_power.append(acc)

    def pupil(i, carry):
        start = pl.multiple_of(i * step, step)
        u = (2.0 * (iota((step, NP), 0) + (i * step).astype(F32)) + 1.0) / NP - 1.0
        turns = jnp.broadcast_to(per_power[DEGREE], (step, NP))
        for power in range(DEGREE - 1, -1, -1):
            turns = turns * u + per_power[power]
        radius = u * u + lane_u * lane_u
        inside = jnp.where((radius <= 1.0) & (radius >= 0.09), 1.0, 0.0)
        real, imag = cos_sin_turns(turns)
        for half, value in enumerate((real * inside, imag * inside)):
            at = (pl.ds(start, step), pl.ds(half * NP, NP))
            high, low = split(value)
            pup[at] = value
            ph[at] = high
            plo[at] = low
        return carry

    lax.fori_loop(0, NP // step, pupil, 0)

    for load in loads:
        load.wait()
    scale = 1.0 / (NR * math.sqrt(nf))
    blocks = rd // 8
    ow[1 : 1 + blocks, 0] = obs_v[...].reshape(blocks, 8, width)
    weight = mask_v[...].astype(F32) * count_v[...].astype(F32) * scale
    ow[1 : 1 + blocks, 1] = weight.reshape(blocks, 8, width)

    @pl.when(b == 0)
    def _():
        maps[0:h] = jnp.zeros((h, 2, k, width), F32)
        ow[0:1] = jnp.zeros((1, 2, 8, width), F32)

    @pl.when(b == nb - 1)
    def _():
        maps[h + nf : 2 * h + nf] = jnp.zeros((h, 2, k, width), F32)
        ow[1 + blocks : 2 + blocks] = jnp.zeros((1, 2, 8, width), F32)

    pl.semaphore_wait(barrier, group - 1)

    def remote(src, dst, send, recv, where):
        return pltpu.make_async_remote_copy(
            src_ref=src, dst_ref=dst, send_sem=send, recv_sem=recv, device_id=where, device_id_type=MESH
        )

    has_up = b > 0
    has_down = b < nb - 1
    gives_down = has_down & (f >= nf - h)
    gives_up = has_up & (f < h)
    mine = maps.at[h + f]

    def ow_up():
        return remote(ow.at[1], ow.at[1 + blocks], ow_send.at[0], ow_recv.at[1], device(f, b - 1))

    def ow_down():
        return remote(ow.at[blocks], ow.at[0], ow_send.at[1], ow_recv.at[0], device(f, b + 1))

    def map_same(i):
        return remote(
            mine, maps.at[h + f], map_send.at[0, i], map_recv.at[h + f], device(lax.rem(f + i + 1, nf), b)
        )

    def map_down(i):
        slot = f - (nf - h)
        return remote(
            mine, maps.at[slot], map_send.at[1, i], map_recv.at[slot], device(lax.rem(f + i, nf), b + 1)
        )

    def map_up(i):
        slot = h + nf + f
        return remote(
            mine, maps.at[slot], map_send.at[2, i], map_recv.at[slot], device(lax.rem(f + i, nf), b - 1)
        )

    repeat(nf - 1, lambda i: map_same(i).start())

    @pl.when(gives_down)
    def _():
        repeat(nf, lambda i: map_down(i).start())

    @pl.when(gives_up)
    def _():
        repeat(nf, lambda i: map_up(i).start())

    @pl.when(has_up)
    def _():
        ow_up().start()

    @pl.when(has_down)
    def _():
        ow_down().start()

    rho = nb * rd / 2.0 + dith[0, 0].astype(F32)
    chi = width / 2.0 + dith[0, 1].astype(F32)
    unit = 1.0 / (2 * OVERSAMPLE * NP)
    col_step = 32

    def column(i, carry):
        start = pl.multiple_of(i * col_step, col_step)
        index = 2.0 * (iota((col_step, width), 0) + (i * col_step).astype(F32)) + (1.0 - NP)
        turns = index * (chi - iota((col_step, width), 1)) * unit
        for half, value in enumerate(cos_sin_turns(turns)):
            at = (pl.ds(start, col_step), pl.ds(half * width, width))
            high, low = split(value)
            bh[at] = high
            bl[at] = low
        return carry

    lax.fori_loop(0, NP // col_step, column, 0)

    sigma = jnp.full((1, width), jit[0], F32)
    inv = 1.0 / sigma
    inv2 = inv * inv
    cube = inv2 * inv

    def blur(i, carry):
        total, total_dot = carry
        start = pl.multiple_of(i * col_step, col_step)
        off = iota((col_step, width), 0) + (i * col_step).astype(F32) - iota((col_step, width), 1)
        square = off * off
        value = jnp.exp(square * (-0.5 * inv2))
        slope = value * (square * cube)
        at = (pl.ds(start, col_step), slice(None))
        gh[at], gl[at] = split(value)
        dh[at], dl[at] = split(slope)
        total = total + jnp.sum(value.reshape(col_step // 8, 8, width), 0)
        total_dot = total_dot + jnp.sum(slope.reshape(col_step // 8, 8, width), 0)
        return total, total_dot

    zero8 = jnp.zeros((8, width), F32)
    total, total_dot = lax.fori_loop(0, width // col_step, blur, (zero8, zero8))
    inv_total = 1.0 / jnp.sum(total, 0, keepdims=True)
    ratio = jnp.sum(total_dot, 0, keepdims=True) * inv_total

    first = (b * rd).astype(F32) - float(HALO)
    row_angle = (2.0 * iota((rows, NP), 1) + (1.0 - NP)) * (rho - first - iota((rows, NP), 0)) * unit
    a_real, a_imag = cos_sin_turns(row_angle)
    left = jnp.concatenate([a_real, a_imag], 0)
    x = dot3(left, ph[...], plo[...])
    mid = jnp.concatenate(
        [x[:rows, :NP] - x[rows:, NP:], x[:rows, NP:] + x[rows:, :NP]], 0
    )
    y = dot3(mid, bh[...], bl[...])
    e_real = y[:rows, :width] - y[rows:, width:]
    e_imag = y[:rows, width:] + y[rows:, :width]
    norm = (AMPLITUDE / NP**2) ** 2
    intensity = (e_real * e_real + e_imag * e_imag) * norm
    own = slice(HALO, HALO + rd)
    blurred = dot3(intensity, gh[...], gl[...]) * inv_total
    blurred_dot = dot3(intensity[own], dh[...], dl[...]) * inv_total - blurred[own] * ratio
    image = blurred + sky[0]

    def arrive(i):
        @pl.when(i != f)
        def _():
            remote(mine, maps.at[h + i], map_send.at[0, 0], map_recv.at[h + i], device(f, b)).wait_recv()

    repeat(nf, arrive)

    @pl.when(has_up)
    def _():
        repeat(h, lambda i: remote(mine, maps.at[i], map_send.at[0, 0], map_recv.at[i], device(f, b)).wait_recv())
        ow_down().wait_recv()

    @pl.when(has_down)
    def _():
        repeat(
            h,
            lambda i: remote(
                mine, maps.at[h + nf + i], map_send.at[0, 0], map_recv.at[h + nf + i], device(f, b)
            ).wait_recv(),
        )
        ow_up().wait_recv()

    flat = maps[:, 0].reshape(rows, width)
    bfe = maps[:, 1].reshape(rows, width)
    observed = ow[:, 0].reshape(rows, width)
    weights = ow[:, 1].reshape(rows, width)
    col = lax.broadcasted_iota(jnp.int32, (rows, width), 1)

    def down(value, d):
        return pltpu.roll(value, (-d) % value.shape[0], 0)

    def across(value, d):
        rolled = pltpu.roll(value, (-d) % width, 1)
        at = col[: value.shape[0]]
        return jnp.where(at < width - d if d > 0 else at >= -d, rolled, 0.0)

    def curve(value):
        one = down(value, 1) + down(value, -1)
        two = down(value, 2) + down(value, -2)
        parts = [BFE[0][j] * value + BFE[1][j] * one + BFE[2][j] * two for j in range(3)]
        return (
            parts[0]
            + (across(parts[1], 1) + across(parts[1], -1))
            + (across(parts[2], 2) + across(parts[2], -2))
        )

    kappa = [[ipc[i, j] + (IPC_CENTER if i == j == 1 else 0.0) for j in range(3)] for i in range(3)]

    def couple(value, table):
        shifted = [down(value, -1), value, down(value, 1)]
        parts = [sum(table[i][j] * shifted[i] for i in range(3)) for j in range(3)]
        return parts[1] + across(parts[0], -1) + across(parts[2], 1)

    charge = flat * image
    curvature = curve(charge)
    gain = 1.0 + bfe * curvature
    spread = charge * gain
    resid = weights * (couple(spread, kappa) - observed)
    spread_grad = couple(resid, [row[::-1] for row in kappa[::-1]])
    scaled = spread_grad * charge
    charge_grad = (spread_grad * gain + curve(scaled * bfe))[own]
    gout[:, 1] = (scaled * curvature)[own].reshape(nf, k, width)
    gout[:, 0] = (charge_grad * image[own]).reshape(nf, k, width)

    def scatter(i):
        other = lax.rem(f + i + 1, nf)
        return remote(gout.at[other], gin.at[f], rs_send.at[i], rs_recv.at[f], device(other, b))

    repeat(nf - 1, lambda i: scatter(i).start())
    gin[f] = gout[f]

    image_grad = charge_grad * flat[own]
    dint = dot3(image_grad * inv_total, gh[...], gl[...]) * (2.0 * norm)
    de = jnp.concatenate([e_real[own] * dint, e_imag[own] * dint], 0)
    nt = ((1,), (1,))
    z_real = dot3(de, bh[:, :width], bl[:, :width], nt)
    z_imag = dot3(de, bh[:, width:], bl[:, width:], nt)
    dm_real = z_real[:rd] + z_imag[rd:]
    dm_imag = z_real[rd:] - z_imag[:rd]
    right = jnp.concatenate(
        [jnp.concatenate([dm_real, dm_imag], 1), jnp.concatenate([dm_imag, -dm_real], 1)], 0
    )
    right_high, right_low = split(right)
    left_own = jnp.concatenate([a_real[own], a_imag[own]], 0).T
    left_high, left_low = split(left_own)
    dp = (
        mm(left_high, right_high) + mm(left_low, right_high) + mm(left_high, right_low)
    )
    dphase = pup[:, :NP] * dp[:, NP:] - pup[:, NP:] * dp[:, :NP]
    full_u = (2.0 * iota((NP, NP), 0) + 1.0) / NP - 1.0
    term = dphase
    by_power = []
    for power in range(DEGREE + 1):
        by_power.append(jnp.sum(term, 0, keepdims=True))
        if power < DEGREE:
            term = term * full_u
    by_power.append(jnp.zeros((2, NP), F32))
    by_row = jnp.concatenate(by_power, 0)
    sub = lax.broadcasted_iota(jnp.int32, (8, 128), 0)
    lane = lax.broadcasted_iota(jnp.int32, (8, 128), 1)
    modes = jnp.zeros((8, 128), F32)
    for q in range(DEGREE + 1):
        value = jnp.sum(by_row * lane_pow[q], 1, keepdims=True)
        for power in range(DEGREE + 1 - q):
            d = power + q
            here = (sub == power) & (lane == d * (d + 1) // 2 + power)
            modes = jnp.where(here, value, modes)
    modes = jnp.sum(modes, 0, keepdims=True)

    def fold(value):
        folded = jnp.sum(value.reshape(rd // 8, 8, width), 0)
        return sum(folded[:, j * 128 : (j + 1) * 128] for j in range(width // 128))

    def everything(folded):
        return jnp.sum(jnp.sum(folded, 0, keepdims=True), 1, keepdims=True)

    tile = jnp.where(sub == 1, modes, 0.0)
    resid_own = resid[own]
    shifted_resid = [across(resid_own, 1), resid_own, across(resid_own, -1)]
    for i in range(3):
        spread_rows = spread[HALO + i - 1 : HALO + rd + i - 1]
        for j in range(3):
            value = everything(fold(shifted_resid[j] * spread_rows))
            tile = jnp.where((sub == 0) & (lane == 3 * i + j), value, tile)
    tile = jnp.where((sub == 2) & (lane == 0), everything(fold(image_grad * blurred_dot)), tile)
    outbox[...] = tile

    def post(i):
        return remote(outbox, inbox.at[me], box_send.at[i], box_recv.at[me], peer(i + 1)[1])

    repeat(group - 1, lambda i: post(i).start())
    inbox[me] = tile

    def gathered(i):
        other = lax.rem(f + i + 1, nf)
        remote(gout.at[0], gin.at[other], rs_send.at[i], rs_recv.at[other], device(other, b)).wait_recv()

    repeat(nf - 1, gathered)
    summed = jnp.sum(gin[...], 0)
    gflat[0] = summed[0]
    gbfe[0] = summed[1]

    def posted(i):
        other, where = peer(i + 1)
        remote(outbox, inbox.at[other], box_send.at[i], box_recv.at[other], where).wait_recv()

    repeat(group - 1, posted)
    of_frame = jnp.sum(inbox[pl.ds(f * nb, nb)], 0)
    small[...] = jnp.where(sub == 2, of_frame, jnp.sum(inbox[...], 0))

    repeat(nf - 1, lambda i: map_same(i).wait_send())

    @pl.when(gives_down)
    def _():
        repeat(nf, lambda i: map_down(i).wait_send())

    @pl.when(gives_up)
    def _():
        repeat(nf, lambda i: map_up(i).wait_send())

    @pl.when(has_up)
    def _():
        ow_up().wait_send()

    @pl.when(has_down)
    def _():
        ow_down().wait_send()

    repeat(nf - 1, lambda i: scatter(i).wait_send())
    repeat(group - 1, lambda i: post(i).wait_send())


def local(
    nf, nmap, npsf,
    observed, pixel_mask, ramp_counts, flat_map, bfe_map, ipc_kernel, zernike, jitter, sky_level, dither,
):
    _, rd, width = observed.shape
    k = flat_map.shape[1]
    group = nf * nmap * npsf
    h = HALO // k
    smem = pl.BlockSpec(memory_space=pltpu.SMEM)
    hbm = pl.BlockSpec(memory_space=pl.ANY)
    vmem = pl.BlockSpec(memory_space=pltpu.VMEM)
    dma = pltpu.SemaphoreType.DMA
    gflat, gbfe, small = pl.pallas_call(
        functools.partial(kernel, nf, nmap, npsf, rd, k, width),
        out_shape=(
            jax.ShapeDtypeStruct((1, k, width), F32),
            jax.ShapeDtypeStruct((1, k, width), F32),
            jax.ShapeDtypeStruct((8, 128), F32),
        ),
        in_specs=[smem] * 5 + [hbm] * 5,
        out_specs=(vmem, vmem, vmem),
        scratch_shapes=[
            pltpu.VMEM((nf + 2 * h, 2, k, width), F32),
            pltpu.VMEM((rd // 8 + 2, 2, 8, width), F32),
            pltpu.VMEM((rd, width), F32),
            pltpu.VMEM((rd, width), jnp.int32),
            pltpu.VMEM((rd, width), jnp.int32),
            pltpu.VMEM((NP, 2 * NP), F32),
            pltpu.VMEM((NP, 2 * NP), BF16),
            pltpu.VMEM((NP, 2 * NP), BF16),
            pltpu.VMEM((NP, 2 * width), BF16),
            pltpu.VMEM((NP, 2 * width), BF16),
            pltpu.VMEM((width, width), BF16),
            pltpu.VMEM((width, width), BF16),
            pltpu.VMEM((width, width), BF16),
            pltpu.VMEM((width, width), BF16),
            pltpu.VMEM((nf, 2, k, width), F32),
            pltpu.VMEM((nf, 2, k, width), F32),
            pltpu.VMEM((8, 128), F32),
            pltpu.VMEM((group, 8, 128), F32),
            dma((5,)),
            dma((3, nf)),
            dma((nf + 2 * h,)),
            dma((2,)),
            dma((2,)),
            dma((nf,)),
            dma((nf,)),
            dma((group,)),
            dma((group,)),
        ],
        compiler_params=pltpu.CompilerParams(
            collective_id=0, has_side_effects=True, vmem_limit_bytes=40 * 1024 * 1024
        ),
    )(zernike, jitter, sky_level, dither, ipc_kernel, flat_map, bfe_map, observed, pixel_mask, ramp_counts)
    return (gflat, gbfe, small[0, :9].reshape(3, 3), small[1, : zernike.shape[0]], small[2, :1])


def solution(mesh):
    in_specs = (
        P(("groups", "frame"), ("map", "psf"), None),
        P(("groups", "frame"), ("map", "psf"), None),
        P(("groups", "frame"), ("map", "psf"), None),
        P(("groups", "map", "psf"), "frame", None),
        P(("groups", "map", "psf"), "frame", None),
        P("groups", None),
        P("groups"),
        P(("groups", "frame")),
        P(("groups", "frame")),
        P(("groups", "frame"), None),
    )
    out_specs = (
        P(("groups", "map", "psf"), "frame", None),
        P(("groups", "map", "psf"), "frame", None),
        P("groups", None),
        P("groups"),
        P(("groups", "frame")),
    )
    body = functools.partial(local, mesh.shape["frame"], mesh.shape["map"], mesh.shape["psf"])
    return jax.shard_map(body, mesh=mesh, in_specs=in_specs, out_specs=out_specs, check_vma=False)
```

profile of v0, /device:TPU:0, one launch (start us, length us, event | category | flops | bytes accessed | tf_op | source)
XLA Modules:
  0.0 28.8 jit_solution(10859136181665530460)
XLA Ops:
  0.6 0.0 copy-start.5
  1.3 0.0 copy-start.6
  1.3 0.0 copy-start.7
  2.0 0.0 copy-done.5
  2.0 0.0 copy-done.6
  2.0 0.0 copy-done.7
  2.0 0.0 copy-start
  2.0 0.8 %copy-done = f32[1,32,512]{2,1,0:T(8,128)S(1)} copy-done((f32[1,32,512]{2,1,0:T(8,128)S(1)}, f32[1,32,512]{2,1,0:T(8,128)}, u32[]{:S(2)}) %copy-start) | copy-done | bytes 65560
  2.9 0.0 copy-start.1
  2.9 0.8 %copy-done.1 = s32[1,32,512]{2,1,0:T(8,128)S(1)} copy-done((s32[1,32,512]{2,1,0:T(8,128)S(1)}, s32[1,32,512]{2,1,0:T(8,128)}, u32[]{:S(2)}) %copy-start.1) | copy-done | bytes 65560
  3.7 0.0 copy-start.2
  3.7 0.8 %copy-done.2 = s32[1,32,512]{2,1,0:T(8,128)S(1)} copy-done((s32[1,32,512]{2,1,0:T(8,128)S(1)}, s32[1,32,512]{2,1,0:T(8,128)}, u32[]{:S(2)}) %copy-start.2) | copy-done | bytes 65560
  4.5 0.0 copy-start.3
  4.5 0.7 %copy-done.3 = f32[1,8,512]{2,1,0:T(8,128)S(1)} copy-done((f32[1,8,512]{2,1,0:T(8,128)S(1)}, f32[1,8,512]{2,1,0:T(8,128)}, u32[]{:S(2)}) %copy-start.3) | copy-done | bytes 16408
  5.3 0.0 copy-start.4
  5.3 0.7 %copy-done.4 = f32[1,8,512]{2,1,0:T(8,128)S(1)} copy-done((f32[1,8,512]{2,1,0:T(8,128)S(1)}, f32[1,8,512]{2,1,0:T(8,128)}, u32[]{:S(2)}) %copy-start.4) | copy-done | bytes 16408
  6.0 19.9 %shard_map.137 = (f32[1,8,512]{2,1,0:T(8,128)S(1)}, f32[1,8,512]{2,1,0:T(8,128)S(1)}, f32[8,128]{1,0:T(8,128)S(1)}) custom-call(f32[21]{0:T(128)S(1)} %copy-done.6, f32[1]{0:T(128)S(6)} %copy.17.jit, f32[1]{0:T(128)S(6)} %copy.18.sky, s32[1,2]{1,0:T(1,128)S(1)} %copy-done.7, f32[3,3]{1,0:T(4,128)S(1)} %copy-done.5, f32[1,8,512]{2,1,0:T(8,128)S(1)} %copy-done.3, ...), custom_call_target="tpu_custom_call" | custom-call | tf_op jit(solution)/shard_map/pallas_call | solution.py:484
  25.9 0.7 %reshape_squeeze.3 = f32[3,3]{1,0:T(4,128)} reshape(f32[9]{0:T(128)S(1)} %slice_reduce_fusion) | data formatting | bytes 72 | tf_op jit(solution)/shard_map/reshape;squeeze | solution.py:526
  26.5 0.5 %slice.11 = f32[1,1]{1,0:T(1,128)} slice(f32[8,128]{1,0:T(8,128)S(1)} %get-tuple-element.10), slice={[2:3], [0:1]} | slice | bytes 8 | tf_op jit(solution)/shard_map/slice | solution.py:526
  27.1 0.5 %slice_bitcast_fusion = f32[21]{0:T(128)} fusion(f32[8,128]{1,0:T(8,128)S(1)} %get-tuple-element.10), kind=kLoop, calls=%fused_computation | loop fusion | bytes 168 | tf_op jit(solution)/shard_map/squeeze | solution.py:526
  27.6 0.6 %copy.19 = f32[1,8,512]{2,1,0:T(8,128)} copy(f32[1,8,512]{2,1,0:T(8,128)S(1)} %get-tuple-element.16) | data formatting | bytes 32768
  28.2 0.6 %copy.20 = f32[1,8,512]{2,1,0:T(8,128)} copy(f32[1,8,512]{2,1,0:T(8,128)S(1)} %get-tuple-element.17) | data formatting | bytes 32768
  (1 shorter events, 0.0 us)
Async XLA Ops:
  0.6 1.4 %copy-start.5 = (f32[3,3]{1,0:T(4,128)S(1)}, f32[3,3]{1,0:T(4,128)}, u32[]{:S(2)}) copy-start(f32[3,3]{1,0:T(4,128)} %ipc.1) | copy-start | bytes 112
  1.3 0.7 %copy-start.6 = (f32[21]{0:T(128)S(1)}, f32[21]{0:T(128)}, u32[]{:S(2)}) copy-start(f32[21]{0:T(128)} %zern.1) | copy-start | bytes 256
  1.3 0.7 %copy-start.7 = (s32[1,2]{1,0:T(1,128)S(1)}, s32[1,2]{1,0:T(1,128)}, u32[]{:S(2)}) copy-start(s32[1,2]{1,0:T(1,128)} %dith.1) | copy-start | bytes 28
  2.0 0.8 %copy-start = (f32[1,32,512]{2,1,0:T(8,128)S(1)}, f32[1,32,512]{2,1,0:T(8,128)}, u32[]{:S(2)}) copy-start(f32[1,32,512]{2,1,0:T(8,128)} %obs_in.1) | copy-start | bytes 196612
  2.9 0.8 %copy-start.1 = (s32[1,32,512]{2,1,0:T(8,128)S(1)}, s32[1,32,512]{2,1,0:T(8,128)}, u32[]{:S(2)}) copy-start(s32[1,32,512]{2,1,0:T(8,128)} %mask_in.1) | copy-start | bytes 196612
  3.7 0.8 %copy-start.2 = (s32[1,32,512]{2,1,0:T(8,128)S(1)}, s32[1,32,512]{2,1,0:T(8,128)}, u32[]{:S(2)}) copy-start(s32[1,32,512]{2,1,0:T(8,128)} %count_in.1) | copy-start | bytes 196612
  4.5 0.7 %copy-start.3 = (f32[1,8,512]{2,1,0:T(8,128)S(1)}, f32[1,8,512]{2,1,0:T(8,128)}, u32[]{:S(2)}) copy-start(f32[1,8,512]{2,1,0:T(8,128)} %flat_in.1) | copy-start | bytes 49156
  5.3 0.7 %copy-start.4 = (f32[1,8,512]{2,1,0:T(8,128)S(1)}, f32[1,8,512]{2,1,0:T(8,128)}, u32[]{:S(2)}) copy-start(f32[1,8,512]{2,1,0:T(8,128)} %bfe_in.1) | copy-start | bytes 49156
where the time goes:
time: 29.2 us; the launch traced here: 28.8 us
  Pallas kernels  19.9 us (68%)
  local copies, waits for them, and re-layouts  6.87 us (24%)
  between operations  2.03 us (7%)
    pallas_call x1, Pallas kernels, local(): pl.pallas_call(functools.partial(kernel, nf, nmap, npsf, rd, k, width), o...  19.9 us
    unnamed x18, local copies, waits for them, and re-layouts  5.17 us
    another operation x1, local copies, waits for them, and re-layouts, local(): small[0, :9].reshape(3, 3)  0.66 us

commit v1 on v0

--- a/solution.py
+++ b/solution.py
@@ -12,6 +12,7 @@
 NP = 256
 NR = 16
 HALO = 8
+VMEM_LIMIT = 63 * 1024 * 1024
 OVERSAMPLE = 32
 AMPLITUDE = 2.0
 IPC_CENTER = 0.8
@@ -94,10 +95,11 @@
 
 def kernel(
     nf, nmap, npsf, rd, k, width,
-    zern, jit, sky, dith, ipc, flat_in, bfe_in, obs_in, mask_in, count_in,
-    gflat, gbfe, small,
+    zern_in, jit_in, sky_in, dith_in, ipc_in, flat_in, bfe_in, obs_in, mask_in, count_in,
+    gsum, small,
+    zern, jit, sky, dith, ipc,
     maps, ow, obs_v, mask_v, count_v, pup, ph, plo, bh, bl, gh, gl, dh, dl, gout, gin, outbox, inbox,
-    local_sem, map_send, map_recv, ow_send, ow_recv, rs_send, rs_recv, box_send, box_recv,
+    local_sem, map_send, pass_send, map_recv, ow_send, ow_recv, rs_send, rs_recv, box_send, box_recv,
 ):
     nb = nmap * npsf
     group = nf * nb
@@ -129,9 +131,75 @@
         pltpu.make_async_copy(obs_in.at[0], obs_v, local_sem.at[2]),
         pltpu.make_async_copy(mask_in.at[0], mask_v, local_sem.at[3]),
         pltpu.make_async_copy(count_in.at[0], count_v, local_sem.at[4]),
+        pltpu.make_async_copy(zern_in, zern, local_sem.at[5]),
+        pltpu.make_async_copy(jit_in, jit, local_sem.at[6]),
+        pltpu.make_async_copy(sky_in, sky, local_sem.at[7]),
+        pltpu.make_async_copy(dith_in, dith, local_sem.at[8]),
+        pltpu.make_async_copy(ipc_in, ipc, local_sem.at[9]),
     ]
     for load in loads:
         load.start()
+
+    def remote(src, dst, send, recv, where):
+        return pltpu.make_async_remote_copy(
+            src_ref=src, dst_ref=dst, send_sem=send, recv_sem=recv, device_id=where, device_id_type=MESH
+        )
+
+    has_up = b > 0
+    has_down = b < nb - 1
+    blocks = rd // 8
+    mine = maps.at[h + f]
+
+    def ow_up():
+        return remote(ow.at[1], ow.at[1 + blocks], ow_send.at[0], ow_recv.at[1], device(f, b - 1))
+
+    def ow_down():
+        return remote(ow.at[blocks], ow.at[0], ow_send.at[1], ow_recv.at[0], device(f, b + 1))
+
+    def map_same(i):
+        return remote(mine, maps.at[h + f], map_send.at[i], map_recv.at[h + f], device(lax.rem(f + i + 1, nf), b))
+
+    def map_down(i):
+        return remote(maps.at[nf + i], maps.at[i], pass_send.at[1, i], map_recv.at[i], device(f, b + 1))
+
+    def map_up(i):
+        slot = h + nf + i
+        return remote(maps.at[h + i], maps.at[slot], pass_send.at[0, i], map_recv.at[slot], device(f, b - 1))
+
+    def arrive(i):
+        @pl.when(i != f)
+        def _():
+            remote(mine, maps.at[h + i], map_send.at[0], map_recv.at[h + i], device(f, b)).wait_recv()
+
+    @pl.when(b == 0)
+    def _():
+        maps[0:h] = jnp.zeros((h, 2, k, width), F32)
+        ow[0:1] = jnp.zeros((1, 2, 8, width), F32)
+
+    @pl.when(b == nb - 1)
+    def _():
+        maps[h + nf : 2 * h + nf] = jnp.zeros((h, 2, k, width), F32)
+        ow[1 + blocks : 2 + blocks] = jnp.zeros((1, 2, 8, width), F32)
+
+    for load in loads[:2]:
+        load.wait()
+    pl.semaphore_wait(barrier, group - 1)
+    repeat(nf - 1, lambda i: map_same(i).start())
+
+    for load in loads[2:]:
+        load.wait()
+    scale = 1.0 / (NR * math.sqrt(nf))
+    ow[1 : 1 + blocks, 0] = obs_v[...].reshape(blocks, 8, width)
+    weight = mask_v[...].astype(F32) * count_v[...].astype(F32) * scale
+    ow[1 : 1 + blocks, 1] = weight.reshape(blocks, 8, width)
+
+    @pl.when(has_up)
+    def _():
+        ow_up().start()
+
+    @pl.when(has_down)
+    def _():
+        ow_down().start()
 
     step = 64
     lane_u = (2.0 * iota((1, NP), 1) + 1.0) / NP - 1.0
@@ -165,78 +233,6 @@
 
     lax.fori_loop(0, NP // step, pupil, 0)
 
-    for load in loads:
-        load.wait()
-    scale = 1.0 / (NR * math.sqrt(nf))
-    blocks = rd // 8
-    ow[1 : 1 + blocks, 0] = obs_v[...].reshape(blocks, 8, width)
-    weight = mask_v[...].astype(F32) * count_v[...].astype(F32) * scale
-    ow[1 : 1 + blocks, 1] = weight.reshape(blocks, 8, width)
-
-    @pl.when(b == 0)
-    def _():
-        maps[0:h] = jnp.zeros((h, 2, k, width), F32)
-        ow[0:1] = jnp.zeros((1, 2, 8, width), F32)
-
-    @pl.when(b == nb - 1)
-    def _():
-        maps[h + nf : 2 * h + nf] = jnp.zeros((h, 2, k, width), F32)
-        ow[1 + blocks : 2 + blocks] = jnp.zeros((1, 2, 8, width), F32)
-
-    pl.semaphore_wait(barrier, group - 1)
-
-    def remote(src, dst, send, recv, where):
-        return pltpu.make_async_remote_copy(
-            src_ref=src, dst_ref=dst, send_sem=send, recv_sem=recv, device_id=where, device_id_type=MESH
-        )
-
-    has_up = b > 0
-    has_down = b < nb - 1
-    gives_down = has_down & (f >= nf - h)
-    gives_up = has_up & (f < h)
-    mine = maps.at[h + f]
-
-    def ow_up():
-        return remote(ow.at[1], ow.at[1 + blocks], ow_send.at[0], ow_recv.at[1], device(f, b - 1))
-
-    def ow_down():
-        return remote(ow.at[blocks], ow.at[0], ow_send.at[1], ow_recv.at[0], device(f, b + 1))
-
-    def map_same(i):
-        return remote(
-            mine, maps.at[h + f], map_send.at[0, i], map_recv.at[h + f], device(lax.rem(f + i + 1, nf), b)
-        )
-
-    def map_down(i):
-        slot = f - (nf - h)
-        return remote(
-            mine, maps.at[slot], map_send.at[1, i], map_recv.at[slot], device(lax.rem(f + i, nf), b + 1)
-        )
-
-    def map_up(i):
-        slot = h + nf + f
-        return remote(
-            mine, maps.at[slot], map_send.at[2, i], map_recv.at[slot], device(lax.rem(f + i, nf), b - 1)
-        )
-
-    repeat(nf - 1, lambda i: map_same(i).start())
-
-    @pl.when(gives_down)
-    def _():
-        repeat(nf, lambda i: map_down(i).start())
-
-    @pl.when(gives_up)
-    def _():
-        repeat(nf, lambda i: map_up(i).start())
-
-    @pl.when(has_up)
-    def _():
-        ow_up().start()
-
-    @pl.when(has_down)
-    def _():
-        ow_down().start()
-
     rho = nb * rd / 2.0 + dith[0, 0].astype(F32)
     chi = width / 2.0 + dith[0, 1].astype(F32)
     unit = 1.0 / (2 * OVERSAMPLE * NP)
@@ -293,20 +289,27 @@
     norm = (AMPLITUDE / NP**2) ** 2
     intensity = (e_real * e_real + e_imag * e_imag) * norm
     own = slice(HALO, HALO + rd)
+
+    repeat(h, arrive)
+    repeat(h, lambda i: arrive(nf - h + i))
+
+    @pl.when(has_up)
+    def _():
+        repeat(h, lambda i: map_up(i).start())
+
+    @pl.when(has_down)
+    def _():
+        repeat(h, lambda i: map_down(i).start())
+
     blurred = dot3(intensity, gh[...], gl[...]) * inv_total
     blurred_dot = dot3(intensity[own], dh[...], dl[...]) * inv_total - blurred[own] * ratio
     image = blurred + sky[0]
 
-    def arrive(i):
-        @pl.when(i != f)
-        def _():
-            remote(mine, maps.at[h + i], map_send.at[0, 0], map_recv.at[h + i], device(f, b)).wait_recv()
-
-    repeat(nf, arrive)
+    repeat(nf - 2 * h, lambda i: arrive(h + i))
 
     @pl.when(has_up)
     def _():
-        repeat(h, lambda i: remote(mine, maps.at[i], map_send.at[0, 0], map_recv.at[i], device(f, b)).wait_recv())
+        repeat(h, lambda i: remote(mine, maps.at[i], map_send.at[0], map_recv.at[i], device(f, b)).wait_recv())
         ow_down().wait_recv()
 
     @pl.when(has_down)
@@ -314,7 +317,7 @@
         repeat(
             h,
             lambda i: remote(
-                mine, maps.at[h + nf + i], map_send.at[0, 0], map_recv.at[h + nf + i], device(f, b)
+                mine, maps.at[h + nf + i], map_send.at[0], map_recv.at[h + nf + i], device(f, b)
             ).wait_recv(),
         )
         ow_up().wait_recv()
@@ -413,15 +416,15 @@
     def everything(folded):
         return jnp.sum(jnp.sum(folded, 0, keepdims=True), 1, keepdims=True)
 
-    tile = jnp.where(sub == 1, modes, 0.0)
+    tile = jnp.where(sub == 3, modes, 0.0)
     resid_own = resid[own]
     shifted_resid = [across(resid_own, 1), resid_own, across(resid_own, -1)]
     for i in range(3):
         spread_rows = spread[HALO + i - 1 : HALO + rd + i - 1]
         for j in range(3):
             value = everything(fold(shifted_resid[j] * spread_rows))
-            tile = jnp.where((sub == 0) & (lane == 3 * i + j), value, tile)
-    tile = jnp.where((sub == 2) & (lane == 0), everything(fold(image_grad * blurred_dot)), tile)
+            tile = jnp.where((sub == i) & (lane == j), value, tile)
+    tile = jnp.where((sub == 4) & (lane == 0), everything(fold(image_grad * blurred_dot)), tile)
     outbox[...] = tile
 
     def post(i):
@@ -436,8 +439,7 @@
 
     repeat(nf - 1, gathered)
     summed = jnp.sum(gin[...], 0)
-    gflat[0] = summed[0]
-    gbfe[0] = summed[1]
+    gsum[...] = summed
 
     def posted(i):
         other, where = peer(i + 1)
@@ -445,28 +447,30 @@
 
     repeat(group - 1, posted)
     of_frame = jnp.sum(inbox[pl.ds(f * nb, nb)], 0)
-    small[...] = jnp.where(sub == 2, of_frame, jnp.sum(inbox[...], 0))
+    small[...] = jnp.where(sub == 4, of_frame, jnp.sum(inbox[...], 0))
 
     repeat(nf - 1, lambda i: map_same(i).wait_send())
 
-    @pl.when(gives_down)
-    def _():
-        repeat(nf, lambda i: map_down(i).wait_send())
-
-    @pl.when(gives_up)
-    def _():
-        repeat(nf, lambda i: map_up(i).wait_send())
-
     @pl.when(has_up)
     def _():
+        repeat(h, lambda i: map_up(i).wait_send())
         ow_up().wait_send()
 
     @pl.when(has_down)
     def _():
+        repeat(h, lambda i: map_down(i).wait_send())
         ow_down().wait_send()
 
     repeat(nf - 1, lambda i: scatter(i).wait_send())
     repeat(group - 1, lambda i: post(i).wait_send())
+
+
+def finish(gsum, small, gflat, gbfe, gipc, gzern, gjit):
+    gflat[0] = gsum[0]
+    gbfe[0] = gsum[1]
+    gipc[...] = small[0:3, 0:3]
+    gzern[...] = small[3, : gzern.shape[0]]
+    gjit[...] = small[4, 0:1]
 
 
 def local(
@@ -477,20 +481,23 @@
     k = flat_map.shape[1]
     group = nf * nmap * npsf
     h = HALO // k
-    smem = pl.BlockSpec(memory_space=pltpu.SMEM)
     hbm = pl.BlockSpec(memory_space=pl.ANY)
     vmem = pl.BlockSpec(memory_space=pltpu.VMEM)
     dma = pltpu.SemaphoreType.DMA
-    gflat, gbfe, small = pl.pallas_call(
+    gsum, small = pl.pallas_call(
         functools.partial(kernel, nf, nmap, npsf, rd, k, width),
         out_shape=(
-            jax.ShapeDtypeStruct((1, k, width), F32),
-            jax.ShapeDtypeStruct((1, k, width), F32),
+            jax.ShapeDtypeStruct((2, k, width), F32),
             jax.ShapeDtypeStruct((8, 128), F32),
         ),
-        in_specs=[smem] * 5 + [hbm] * 5,
-        out_specs=(vmem, vmem, vmem),
+        in_specs=[hbm] * 10,
+        out_specs=(vmem, vmem),
         scratch_shapes=[
+            pltpu.SMEM(zernike.shape, F32),
+            pltpu.SMEM((1,), F32),
+            pltpu.SMEM((1,), F32),
+            pltpu.SMEM((1, 2), jnp.int32),
+            pltpu.SMEM((3, 3), F32),
             pltpu.VMEM((nf + 2 * h, 2, k, width), F32),
             pltpu.VMEM((rd // 8 + 2, 2, 8, width), F32),
             pltpu.VMEM((rd, width), F32),
@@ -509,8 +516,9 @@
             pltpu.VMEM((nf, 2, k, width), F32),
             pltpu.VMEM((8, 128), F32),
             pltpu.VMEM((group, 8, 128), F32),
-            dma((5,)),
-            dma((3, nf)),
+            dma((10,)),
+            dma((nf,)),
+            dma((2, h)),
             dma((nf + 2 * h,)),
             dma((2,)),
             dma((2,)),
@@ -520,10 +528,21 @@
             dma((group,)),
         ],
         compiler_params=pltpu.CompilerParams(
-            collective_id=0, has_side_effects=True, vmem_limit_bytes=40 * 1024 * 1024
+            collective_id=0, has_side_effects=True, vmem_limit_bytes=VMEM_LIMIT
         ),
     )(zernike, jitter, sky_level, dither, ipc_kernel, flat_map, bfe_map, observed, pixel_mask, ramp_counts)
-    return (gflat, gbfe, small[0, :9].reshape(3, 3), small[1, : zernike.shape[0]], small[2, :1])
+    return pl.pallas_call(
+        finish,
+        out_shape=(
+            jax.ShapeDtypeStruct(flat_map.shape, F32),
+            jax.ShapeDtypeStruct(bfe_map.shape, F32),
+            jax.ShapeDtypeStruct(ipc_kernel.shape, F32),
+            jax.ShapeDtypeStruct(zernike.shape, F32),
+            jax.ShapeDtypeStruct(jitter.shape, F32),
+        ),
+        in_specs=[vmem] * 2,
+        out_specs=(vmem,) * 5,
+    )(gsum, small)
 
 
 def solution(mesh):

time: 29.2 us -> 23.7 us (0.81)
  local copies, waits for them, and re-layouts: 6.87 us -> 0 us
  Pallas kernels: 19.9 us -> 21.5 us
    unnamed x18 -> x0, local copies, waits for them, and re-layouts: 5.17 us -> none
    pallas_call x0 -> x1, Pallas kernels: none -> 1.38 us  [local(): pl.pallas_call(finish, out_shape=(jax.ShapeDtypeStruct(flat_map.shape, F3...]
    another operation x1 -> x0, local copies, waits for them, and re-layouts: 0.66 us -> none  [local(): small[0, :9].reshape(3, 3)]
    slice x2 -> x0, local copies, waits for them, and re-layouts: 0.53 us -> none  [the longest x1 0.51 us: local(): small[2, :1]]
    squeeze x1 -> x0, local copies, waits for them, and re-layouts: 0.51 us -> none  [local(): small[1, :zernike.shape[0]]]
where the time goes in v1:
time: 23.7 us; the launch traced here: 23.4 us
  Pallas kernels  21.5 us (91%)
  between operations  1.93 us (8%)
    pallas_call x1, Pallas kernels, local(): pl.pallas_call(functools.partial(kernel, nf, nmap, npsf, rd, k, width), o...  20.1 us
    pallas_call x1, Pallas kernels, local(): pl.pallas_call(finish, out_shape=(jax.ShapeDtypeStruct(flat_map.shape, F3...  1.38 us

profile of v1, /device:TPU:0, one launch (start us, length us, event | category | flops | bytes accessed | tf_op | source)
XLA Modules:
  0.0 23.4 jit_solution(1490328249191171687)
XLA Ops:
  1.9 20.1 %shard_map.137 = (f32[2,8,512]{2,1,0:T(8,128)}, f32[8,128]{1,0:T(8,128)}) custom-call(f32[21]{0:T(128)} %zern_in.1, f32[1]{0:T(128)S(6)} %copy.15.jit_in, f32[1]{0:T(128)S(6)} %copy.16.sky_in, s32[1,2]{1,0:T(1,128)} %dith_in.1, f32[3,3]{1,0:T(4,128)} %ipc_in.1, f32[1,8,512]{2,1,0:T(8,128)} %flat_in.1, f32[1,8,512]{2,1,0:T(8,128)} %bfe_in.1, ...), custom_call_target="tpu_custom_call" | custom-call | tf_op jit(solution)/shard_map/pallas_call | solution.py:487
  22.1 1.4 %shard_map.138 = (f32[1,8,512]{2,1,0:T(8,128)}, f32[1,8,512]{2,1,0:T(8,128)}, f32[3,3]{1,0:T(4,128)}, f32[21]{0:T(128)}, f32[1]{0:T(128)}) custom-call(f32[2,8,512]{2,1,0:T(8,128)} %get-tuple-element.7.gsum, f32[8,128]{1,0:T(8,128)} %get-tuple-element.8.small), custom_call_target="tpu_custom_call" | custom-call | tf_op jit(solution)/shard_map/pallas_call | solution.py:534

commit v2 on v1

--- a/solution.py
+++ b/solution.py
@@ -95,9 +95,9 @@
 
 def kernel(
     nf, nmap, npsf, rd, k, width,
-    zern_in, jit_in, sky_in, dith_in, ipc_in, flat_in, bfe_in, obs_in, mask_in, count_in,
+    zern_in, level_in, dith_in, ipc_in, flat_in, bfe_in, obs_in, mask_in, count_in,
     gsum, small,
-    zern, jit, sky, dith, ipc,
+    zern, level, dith, ipc,
     maps, ow, obs_v, mask_v, count_v, pup, ph, plo, bh, bl, gh, gl, dh, dl, gout, gin, outbox, inbox,
     local_sem, map_send, pass_send, map_recv, ow_send, ow_recv, rs_send, rs_recv, box_send, box_recv,
 ):
@@ -112,18 +112,23 @@
     me = f * nb + b
 
     def device(frame, block):
-        return {"frame": frame, "map": block // npsf, "psf": block % npsf}
-
-    def peer(offset):
-        other = lax.rem(me + offset, group)
-        return other, device(other // nb, other % nb)
+        return {"frame": frame, "map": lax.div(block, npsf), "psf": lax.rem(block, npsf)}
+
+    def wrap(value, count):
+        return jnp.where(value >= count, value - count, value)
+
+    others = [(i, j) for i in range(nmap) for j in range(npsf)]
+
+    def each_peer(body):
+        def of_frame(step, spots):
+            for i, j in spots:
+                body({"frame": wrap(f + step, nf), "map": wrap(m + i, nmap), "psf": wrap(p + j, npsf)})
+
+        repeat(nf - 1, lambda step: of_frame(step + 1, others))
+        of_frame(0, others[1:])
 
     barrier = pltpu.get_barrier_semaphore()
-
-    def greet(i):
-        pl.semaphore_signal(barrier, inc=1, device_id=peer(i + 1)[1], device_id_type=MESH)
-
-    repeat(group - 1, greet)
+    each_peer(lambda where: pl.semaphore_signal(barrier, inc=1, device_id=where, device_id_type=MESH))
 
     loads = [
         pltpu.make_async_copy(flat_in.at[0], maps.at[h + f, 0], local_sem.at[0]),
@@ -132,10 +137,9 @@
         pltpu.make_async_copy(mask_in.at[0], mask_v, local_sem.at[3]),
         pltpu.make_async_copy(count_in.at[0], count_v, local_sem.at[4]),
         pltpu.make_async_copy(zern_in, zern, local_sem.at[5]),
-        pltpu.make_async_copy(jit_in, jit, local_sem.at[6]),
-        pltpu.make_async_copy(sky_in, sky, local_sem.at[7]),
-        pltpu.make_async_copy(dith_in, dith, local_sem.at[8]),
-        pltpu.make_async_copy(ipc_in, ipc, local_sem.at[9]),
+        pltpu.make_async_copy(level_in, level, local_sem.at[6]),
+        pltpu.make_async_copy(dith_in, dith, local_sem.at[7]),
+        pltpu.make_async_copy(ipc_in, ipc, local_sem.at[8]),
     ]
     for load in loads:
         load.start()
@@ -251,7 +255,7 @@
 
     lax.fori_loop(0, NP // col_step, column, 0)
 
-    sigma = jnp.full((1, width), jit[0], F32)
+    sigma = jnp.full((1, width), level[0], F32)
     inv = 1.0 / sigma
     inv2 = inv * inv
     cube = inv2 * inv
@@ -303,7 +307,7 @@
 
     blurred = dot3(intensity, gh[...], gl[...]) * inv_total
     blurred_dot = dot3(intensity[own], dh[...], dl[...]) * inv_total - blurred[own] * ratio
-    image = blurred + sky[0]
+    image = blurred + level[1]
 
     repeat(nf - 2 * h, lambda i: arrive(h + i))
 
@@ -427,10 +431,7 @@
     tile = jnp.where((sub == 4) & (lane == 0), everything(fold(image_grad * blurred_dot)), tile)
     outbox[...] = tile
 
-    def post(i):
-        return remote(outbox, inbox.at[me], box_send.at[i], box_recv.at[me], peer(i + 1)[1])
-
-    repeat(group - 1, lambda i: post(i).start())
+    each_peer(lambda where: remote(outbox, inbox.at[me], box_send, box_recv, where).start())
     inbox[me] = tile
 
     def gathered(i):
@@ -441,11 +442,9 @@
     summed = jnp.sum(gin[...], 0)
     gsum[...] = summed
 
-    def posted(i):
-        other, where = peer(i + 1)
-        remote(outbox, inbox.at[other], box_send.at[i], box_recv.at[other], where).wait_recv()
-
-    repeat(group - 1, posted)
+    every = inbox.at[pl.ds(0, group - 1)]
+    all_tiles = remote(every, every, box_send, box_recv, device(f, b))
+    all_tiles.wait_recv()
     of_frame = jnp.sum(inbox[pl.ds(f * nb, nb)], 0)
     small[...] = jnp.where(sub == 4, of_frame, jnp.sum(inbox[...], 0))
 
@@ -462,7 +461,7 @@
         ow_down().wait_send()
 
     repeat(nf - 1, lambda i: scatter(i).wait_send())
-    repeat(group - 1, lambda i: post(i).wait_send())
+    all_tiles.wait_send()
 
 
 def finish(gsum, small, gflat, gbfe, gipc, gzern, gjit):
@@ -481,7 +480,7 @@
     k = flat_map.shape[1]
     group = nf * nmap * npsf
     h = HALO // k
-    hbm = pl.BlockSpec(memory_space=pl.ANY)
+    hbm = pl.BlockSpec(memory_space=pltpu.HBM)
     vmem = pl.BlockSpec(memory_space=pltpu.VMEM)
     dma = pltpu.SemaphoreType.DMA
     gsum, small = pl.pallas_call(
@@ -490,12 +489,11 @@
             jax.ShapeDtypeStruct((2, k, width), F32),
             jax.ShapeDtypeStruct((8, 128), F32),
         ),
-        in_specs=[hbm] * 10,
+        in_specs=[hbm] * 9,
         out_specs=(vmem, vmem),
         scratch_shapes=[
             pltpu.SMEM(zernike.shape, F32),
-            pltpu.SMEM((1,), F32),
-            pltpu.SMEM((1,), F32),
+            pltpu.SMEM((2,), F32),
             pltpu.SMEM((1, 2), jnp.int32),
             pltpu.SMEM((3, 3), F32),
             pltpu.VMEM((nf + 2 * h, 2, k, width), F32),
@@ -516,7 +514,7 @@
             pltpu.VMEM((nf, 2, k, width), F32),
             pltpu.VMEM((8, 128), F32),
             pltpu.VMEM((group, 8, 128), F32),
-            dma((10,)),
+            dma((9,)),
             dma((nf,)),
             dma((2, h)),
             dma((nf + 2 * h,)),
@@ -524,13 +522,13 @@
             dma((2,)),
             dma((nf,)),
             dma((nf,)),
-            dma((group,)),
-            dma((group,)),
+            dma,
+            dma,
         ],
         compiler_params=pltpu.CompilerParams(
             collective_id=0, has_side_effects=True, vmem_limit_bytes=VMEM_LIMIT
         ),
-    )(zernike, jitter, sky_level, dither, ipc_kernel, flat_map, bfe_map, observed, pixel_mask, ramp_counts)
+    )(zernike, jnp.concatenate([jitter, sky_level]), dither, ipc_kernel, flat_map, bfe_map, observed, pixel_mask, ramp_counts)
     return pl.pallas_call(
         finish,
         out_shape=(

time: 23.7 us -> 24 us (1.013)
  other arithmetic: 0 us -> 0.59 us
  Pallas kernels: 21.5 us -> 21.2 us
    concatenate x0 -> x1, other arithmetic: none -> 0.59 us  [local(): jnp.concatenate([jitter, sky_level])]
    pallas_call x1, Pallas kernels: 20.1 us -> 19.8 us  [local(): pl.pallas_call(functools.partial(kernel, nf, nmap, npsf, rd, k, width), o...]
where the time goes in v2:
time: 24 us; the launch traced here: 23.7 us
  Pallas kernels  21.2 us (88%)
  between operations  1.93 us (8%)
  other arithmetic  0.59 us (2%)
    pallas_call x1, Pallas kernels, local(): pl.pallas_call(functools.partial(kernel, nf, nmap, npsf, rd, k, width), o...  19.8 us
    pallas_call x1, Pallas kernels, local(): pl.pallas_call(finish, out_shape=(jax.ShapeDtypeStruct(flat_map.shape, F3...  1.38 us
    concatenate x1, other arithmetic, local(): jnp.concatenate([jitter, sky_level])  0.59 us

profile of v2, /device:TPU:0, one launch (start us, length us, event | category | flops | bytes accessed | tf_op | source)
XLA Modules:
  0.0 23.7 jit_solution(12424405389346274464)
XLA Ops:
  1.9 0.6 %pad_maximum_fusion.level_in = f32[2]{0:T(128)} fusion(f32[1]{0:T(128)S(6)} %copy.16, f32[1]{0:T(128)S(6)} %copy.15), kind=kLoop, calls=%fused_computation | loop fusion | flops 2 | bytes 16 | tf_op jit(solution)/shard_map/concatenate | solution.py:531
  2.5 19.8 %shard_map.137 = (f32[2,8,512]{2,1,0:T(8,128)}, f32[8,128]{1,0:T(8,128)}) custom-call(f32[21]{0:T(128)} %zern_in.1, f32[2]{0:T(128)} %pad_maximum_fusion.level_in, s32[1,2]{1,0:T(1,128)} %dith_in.1, f32[3,3]{1,0:T(4,128)} %ipc_in.1, f32[1,8,512]{2,1,0:T(8,128)} %flat_in.1, f32[1,8,512]{2,1,0:T(8,128)} %bfe_in.1, f32[1,32,512]{2,1,0:T(8,128)} %obs_in.1, ...), custom_call_target="tpu_custom_call" | custom-call | tf_op jit(solution)/shard_map/pallas_call | solution.py:486
  22.3 1.4 %shard_map.138 = (f32[1,8,512]{2,1,0:T(8,128)}, f32[1,8,512]{2,1,0:T(8,128)}, f32[3,3]{1,0:T(4,128)}, f32[21]{0:T(128)}, f32[1]{0:T(128)}) custom-call(f32[2,8,512]{2,1,0:T(8,128)} %get-tuple-element.7.gsum, f32[8,128]{1,0:T(8,128)} %get-tuple-element.8.small), custom_call_target="tpu_custom_call" | custom-call | tf_op jit(solution)/shard_map/pallas_call | solution.py:532

commit v3 on v2

--- a/solution.py
+++ b/solution.py
@@ -95,9 +95,9 @@
 
 def kernel(
     nf, nmap, npsf, rd, k, width,
-    zern_in, level_in, dith_in, ipc_in, flat_in, bfe_in, obs_in, mask_in, count_in,
+    zern_in, jit_in, sky_in, dith_in, ipc_in, flat_in, bfe_in, obs_in, mask_in, count_in,
     gsum, small,
-    zern, level, dith, ipc,
+    zern, jit, sky, dith, ipc,
     maps, ow, obs_v, mask_v, count_v, pup, ph, plo, bh, bl, gh, gl, dh, dl, gout, gin, outbox, inbox,
     local_sem, map_send, pass_send, map_recv, ow_send, ow_recv, rs_send, rs_recv, box_send, box_recv,
 ):
@@ -137,9 +137,10 @@
         pltpu.make_async_copy(mask_in.at[0], mask_v, local_sem.at[3]),
         pltpu.make_async_copy(count_in.at[0], count_v, local_sem.at[4]),
         pltpu.make_async_copy(zern_in, zern, local_sem.at[5]),
-        pltpu.make_async_copy(level_in, level, local_sem.at[6]),
-        pltpu.make_async_copy(dith_in, dith, local_sem.at[7]),
-        pltpu.make_async_copy(ipc_in, ipc, local_sem.at[8]),
+        pltpu.make_async_copy(jit_in, jit, local_sem.at[6]),
+        pltpu.make_async_copy(sky_in, sky, local_sem.at[7]),
+        pltpu.make_async_copy(dith_in, dith, local_sem.at[8]),
+        pltpu.make_async_copy(ipc_in, ipc, local_sem.at[9]),
     ]
     for load in loads:
         load.start()
@@ -255,7 +256,7 @@
 
     lax.fori_loop(0, NP // col_step, column, 0)
 
-    sigma = jnp.full((1, width), level[0], F32)
+    sigma = jnp.full((1, width), jit[0], F32)
     inv = 1.0 / sigma
     inv2 = inv * inv
     cube = inv2 * inv
@@ -307,7 +308,7 @@
 
     blurred = dot3(intensity, gh[...], gl[...]) * inv_total
     blurred_dot = dot3(intensity[own], dh[...], dl[...]) * inv_total - blurred[own] * ratio
-    image = blurred + level[1]
+    image = blurred + sky[0]
 
     repeat(nf - 2 * h, lambda i: arrive(h + i))
 
@@ -489,11 +490,12 @@
             jax.ShapeDtypeStruct((2, k, width), F32),
             jax.ShapeDtypeStruct((8, 128), F32),
         ),
-        in_specs=[hbm] * 9,
+        in_specs=[hbm] * 10,
         out_specs=(vmem, vmem),
         scratch_shapes=[
             pltpu.SMEM(zernike.shape, F32),
-            pltpu.SMEM((2,), F32),
+            pltpu.SMEM((1,), F32),
+            pltpu.SMEM((1,), F32),
             pltpu.SMEM((1, 2), jnp.int32),
             pltpu.SMEM((3, 3), F32),
             pltpu.VMEM((nf + 2 * h, 2, k, width), F32),
@@ -514,7 +516,7 @@
             pltpu.VMEM((nf, 2, k, width), F32),
             pltpu.VMEM((8, 128), F32),
             pltpu.VMEM((group, 8, 128), F32),
-            dma((9,)),
+            dma((10,)),
             dma((nf,)),
             dma((2, h)),
             dma((nf + 2 * h,)),
@@ -528,7 +530,7 @@
         compiler_params=pltpu.CompilerParams(
             collective_id=0, has_side_effects=True, vmem_limit_bytes=VMEM_LIMIT
         ),
-    )(zernike, jnp.concatenate([jitter, sky_level]), dither, ipc_kernel, flat_map, bfe_map, observed, pixel_mask, ramp_counts)
+    )(zernike, jitter, sky_level, dither, ipc_kernel, flat_map, bfe_map, observed, pixel_mask, ramp_counts)
     return pl.pallas_call(
         finish,
         out_shape=(

time: 24 us -> 23.5 us (0.979)
  other arithmetic: 0.59 us -> 0 us
    concatenate x1 -> x0, other arithmetic: 0.59 us -> none  [local(): jnp.concatenate([jitter, sky_level])]
where the time goes in v3:
time: 23.5 us; the launch traced here: 23.2 us
  Pallas kernels  21.3 us (91%)
  between operations  1.93 us (8%)
    pallas_call x1, Pallas kernels, local(): pl.pallas_call(functools.partial(kernel, nf, nmap, npsf, rd, k, width), o...  19.9 us
    pallas_call x1, Pallas kernels, local(): pl.pallas_call(finish, out_shape=(jax.ShapeDtypeStruct(flat_map.shape, F3...  1.38 us

profile of v3, /device:TPU:0, one launch (start us, length us, event | category | flops | bytes accessed | tf_op | source)
XLA Modules:
  0.0 23.2 jit_solution(2142981953401908427)
XLA Ops:
  1.9 19.9 %shard_map.137 = (f32[2,8,512]{2,1,0:T(8,128)}, f32[8,128]{1,0:T(8,128)}) custom-call(f32[21]{0:T(128)} %zern_in.1, f32[1]{0:T(128)S(6)} %copy.15.jit_in, f32[1]{0:T(128)S(6)} %copy.16.sky_in, s32[1,2]{1,0:T(1,128)} %dith_in.1, f32[3,3]{1,0:T(4,128)} %ipc_in.1, f32[1,8,512]{2,1,0:T(8,128)} %flat_in.1, f32[1,8,512]{2,1,0:T(8,128)} %bfe_in.1, ...), custom_call_target="tpu_custom_call" | custom-call | tf_op jit(solution)/shard_map/pallas_call | solution.py:487
  21.8 1.4 %shard_map.138 = (f32[1,8,512]{2,1,0:T(8,128)}, f32[1,8,512]{2,1,0:T(8,128)}, f32[3,3]{1,0:T(4,128)}, f32[21]{0:T(128)}, f32[1]{0:T(128)}) custom-call(f32[2,8,512]{2,1,0:T(8,128)} %get-tuple-element.7.gsum, f32[8,128]{1,0:T(8,128)} %get-tuple-element.8.small), custom_call_target="tpu_custom_call" | custom-call | tf_op jit(solution)/shard_map/pallas_call | solution.py:534
